TPU v7x, 128 devices: a whole 4x4x4 slice. The times are simulated.
128 devices in a mesh: tm: 8 (over y_lo, z), space: 16 (over y_hi, x, core).
Axes of the slice: x: 4, y: 4 (y_hi: 2, y_lo: 2; y = y_hi * 2 + y_lo), z: 4, core: 2. Of those that a mesh axis runs over, the one named last changes fastest.
Arguments:
- snapshots: bfloat16 [1024, 786432], P('tm', 'space'), may hold values from -10 to 10, as said below
- area_weight: float32 [786432], P('space'), may hold values from 0.1 to 1
- eigvecs: bfloat16 [1024, 64], replicated, may hold values from -0.1875 to 0.1875
- eigvals: float32 [64], replicated, may hold values from 0.5 to 8
Outputs:
- gram: float32 [1024, 1024], P(('tm', 'space'))
- modes: bfloat16 [64, 786432], P('tm', 'space')
Inputs may be any that keep to these rules, and one draw needn't show every extreme that they name: `snapshots`: a per-column climatology plus hourly departures.
All inputs are finite; a program needn't handle non-finite values.
Results may differ from a plain program's by a relative error of at most 0.01.
Values may be sent and summed in bfloat16 or wider, within the bound.
A program may use at most 128 MiB of HBM per device.

v0:
```python
import jax
import jax.numpy as jnp
from jax import lax
from jax.sharding import PartitionSpec as P


def gram_local(weighted):
    return lax.dot_general(
        weighted, weighted, (((1,), (1,)), ((), ())), preferred_element_type=jnp.float32
    )


def local(snapshots, area_weight, eigvecs, eigvals):
    tm_count = lax.axis_size("tm")
    space_count = lax.axis_size("space")
    time_dev, cell_dev = snapshots.shape
    times = time_dev * tm_count
    cells = cell_dev * space_count
    sub_cells = cell_dev // tm_count
    mode_count = eigvecs.shape[1]
    mode_dev = mode_count // tm_count
    tm_index = lax.axis_index("tm")
    columns = lax.all_to_all(snapshots, "tm", split_axis=1, concat_axis=0, tiled=True)
    mean = jnp.sum(columns.astype(jnp.float32), axis=0) / times
    root = jnp.sqrt(area_weight)
    own_root = lax.dynamic_slice_in_dim(root, tm_index * sub_cells, sub_cells, 0)
    weighted = (own_root[None, :] * (columns.astype(jnp.float32) - mean[None, :])).astype(
        jnp.bfloat16
    )
    partial_gram = gram_local(weighted) / cells
    row_sums = lax.psum_scatter(
        partial_gram.astype(jnp.bfloat16), "tm", scatter_dimension=0, tiled=True
    )
    gram = lax.psum_scatter(row_sums, "space", scatter_dimension=0, tiled=True).astype(jnp.float32)
    inv_root = 1.0 / jnp.sqrt(eigvals)
    all_means = lax.all_gather(mean, "tm", axis=0, tiled=True)
    local_weighted = (root[None, :] * (snapshots.astype(jnp.float32) - all_means[None, :])).astype(
        jnp.bfloat16
    )
    own_rows = lax.dynamic_slice_in_dim(eigvecs, tm_index * time_dev, time_dev, 0)
    summed = lax.psum_scatter(
        jnp.dot(own_rows.T, local_weighted, preferred_element_type=jnp.float32),
        "tm",
        scatter_dimension=0,
        tiled=True,
    )
    own_scale = lax.dynamic_slice_in_dim(inv_root, tm_index * mode_dev, mode_dev, 0)
    modes = (summed * own_scale[:, None]).astype(jnp.bfloat16)
    return (gram, modes)


def solution(mesh):
    in_specs = (P("tm", "space"), P("space"), P(), P())
    out_specs = (P(("tm", "space"), None), P("tm", "space"))
    return jax.shard_map(local, mesh=mesh, in_specs=in_specs, out_specs=out_specs, check_vma=False)
```

profile of v0, /device:TPU:1, one launch (start us, length us, event | category | flops | bytes accessed | tf_op | source)
XLA Modules:
  0.0 477.4 jit_solution(4174322892892114167)
XLA Ops:
  7.2 0.0 copy-start
  7.2 16.5 %copy.8 = bf16[128,49152]{0,1:T(8,128)(2,1)} copy(bf16[128,49152]{1,0:T(8,128)(2,1)} %param.4) | data formatting | bytes 25165824 | tf_op args[0]
  23.7 0.0 copy-start.1
  23.7 7.0 %all-to-all-start = ((bf16[128,8,6144]{0,2,1:T(8,128)(2,1)}), bf16[128,8,6144]{0,2,1:T(8,128)(2,1)}, u32[]{:S(2)}, u32[]{:S(2)}) async-start(bf16[128,8,6144]{0,2,1:T(8,128)(2,1)} %bitcast.6), calls=%async_computation | async-start | bytes 25165824 | tf_op jit(solution)/shard_map/all_to_all | solution.py:23
  30.7 0.0 reduce-scatter.4.cloned.1.call-start
  30.7 0.0 copy-done.1
  30.7 0.1 sqrt.6
  30.8 139.1 %all-to-all-done = bf16[128,8,6144]{0,2,1:T(8,128)(2,1)} async-done(((bf16[128,8,6144]{0,2,1:T(8,128)(2,1)}), bf16[128,8,6144]{0,2,1:T(8,128)(2,1)}, u32[]{:S(2)}, u32[]{:S(2)}) %all-to-all-start) | async-done | bytes 12582944 | tf_op jit(solution)/shard_map/all_to_all | solution.py:23
  169.9 6.3 %convert_reduce_fusion = f32[6144]{0:T(1024)S(1)} fusion(bf16[128,8,6144]{0,2,1:T(8,128)(2,1)} %all-to-all-done), kind=kLoop, calls=%fused_computation.1 | loop fusion | flops 12576768 | bytes 12607488 | tf_op jit(solution)/shard_map/reduce_sum | solution.py:24
  176.2 11.9 %fusion.3 = bf16[8,128,6144]{1,2,0:T(8,128)(2,1)} fusion(bf16[128,8,6144]{0,2,1:T(8,128)(2,1)} %all-to-all-done, f32[6144]{0:T(1024)S(1)} %broadcast_multiply_fusion, f32[6144]{0:T(1024)S(1)} %dynamic_slice.9), kind=kLoop, calls=%fused_computation.6 | loop fusion | flops 25165824 | bytes 25214976 | tf_op jit(solution)/shard_map/convert_element_type | solution.py:27
  188.1 16.7 %copy.9 = bf16[8,128,6144]{2,1,0:T(8,128)(2,1)} copy(bf16[8,128,6144]{1,2,0:T(8,128)(2,1)} %fusion.3) | data formatting | bytes 25165824 | tf_op jit(solution)/shard_map/convert_element_type | solution.py:27
  204.8 19.1 %multiply_convert_fusion.2 = bf16[1024,1024]{1,0:T(8,128)(2,1)} fusion(bf16[1024,6144]{1,0:T(8,128)(2,1)} %bitcast.7), kind=kOutput, calls=%fused_computation.9 | convolution fusion | flops 12886999040 | bytes 14680064 | tf_op jit(solution)/shard_map/dot_general | solution.py:8
  223.8 0.0 reduce-scatter.4.cloned.1.call-update
  223.9 0.0 reduce-scatter.6.cloned.1.call-start
  223.9 23.4 %all_gather.3 = f32[49152]{0:T(1024)S(1)} all-gather(f32[6144]{0:T(1024)S(1)} %broadcast_multiply_fusion), channel_id=1, replica_groups=mesh['tm'=8,'space'=16] {'tm'}, dimensions={0}, use_global_device_ids=true | all-gather | bytes 221184 | tf_op jit(solution)/shard_map/all_gather | solution.py:36
  247.3 14.6 %reduce-scatter.4.cloned.1.call-done = bf16[128,1024]{1,0:T(8,128)(2,1)} async-done(((bf16[1024,1024]{1,0:T(8,128)(2,1)}), bf16[128,1024]{1,0:T(8,128)(2,1)}) %reduce-scatter.4.cloned.1.call-update) | async-done | bytes 262160 | tf_op jit(solution)/shard_map/reduce_scatter | solution.py:31
  261.9 0.0 reduce-scatter.6.cloned.1.call-update
  261.9 0.0 reduce-scatter.8.cloned.1.call-start
  262.0 0.0 copy-done
  262.0 13.2 %fusion.2 = f32[64,49152]{1,0:T(8,128)} fusion(bf16[128,49152]{1,0:T(8,128)(2,1)} %param.4, f32[49152]{0:T(1024)S(1)} %all_gather.3, f32[49152]{0:T(1024)S(1)} %sqrt.6, bf16[1024,64]{0,1:T(8,128)(2,1)S(1)} %copy-done, s32[]{:T(128)S(6)} %select_n.10), kind=kOutput, calls=%fused_computation.5 | convolution fusion | flops 830472192 | bytes 25575428 | tf_op jit(solution)/shard_map/dot_general | solution.py:42
  275.2 0.0 copy-start.2
  275.2 0.0 reduce-scatter.8.cloned.1.call-update
  275.2 0.6 copy-done.2
  275.8 0.1 dynamic_slice.11
  275.9 56.3 %reduce-scatter.6.cloned.1.call-done = bf16[8,1024]{1,0:T(8,128)(2,1)} async-done(((bf16[128,1024]{1,0:T(8,128)(2,1)}), bf16[8,1024]{1,0:T(8,128)(2,1)}) %reduce-scatter.6.cloned.1.call-update) | async-done | bytes 16400 | tf_op jit(solution)/shard_map/reduce_scatter | solution.py:34
  332.2 1.3 convert_element_type.38
  333.6 134.8 %reduce-scatter.8.cloned.1.call-done = f32[8,49152]{1,0:T(8,128)} async-done(((f32[64,49152]{1,0:T(8,128)}), f32[8,49152]{1,0:T(8,128)}) %reduce-scatter.8.cloned.1.call-update) | async-done | bytes 1572880 | tf_op jit(solution)/shard_map/reduce_scatter | solution.py:41
  468.4 2.4 multiply_convert_fusion.3
  (3 shorter events, 0.0 us)
Async XLA Ops:
  7.2 254.8 %copy-start = (bf16[1024,64]{0,1:T(8,128)(2,1)S(1)}, bf16[1024,64]{0,1:T(8,128)(2,1)}, u32[]{:S(2)}) copy-start(bf16[1024,64]{0,1:T(8,128)(2,1)} %param.6) | copy-start | bytes 393220
  23.7 7.1 %copy-start.1 = (f32[49152]{0:T(1024)S(1)}, f32[49152]{0:T(1024)}, u32[]{:S(2)}) copy-start(f32[49152]{0:T(1024)} %param.5) | copy-start | bytes 589828
  23.7 146.3 %all-to-all-start = ((bf16[128,8,6144]{0,2,1:T(8,128)(2,1)}), bf16[128,8,6144]{0,2,1:T(8,128)(2,1)}, u32[]{:S(2)}, u32[]{:S(2)}) async-start(bf16[128,8,6144]{0,2,1:T(8,128)(2,1)} %bitcast.6), calls=%async_computation | async-start | bytes 25165824 | tf_op jit(solution)/shard_map/all_to_all | solution.py:23
  30.7 231.2 %reduce-scatter.4.cloned.1.call-start = ((), (), s32[]{:S(2)}) async-start(), calls=%async_computation.4 | async-start | bytes 2359296 | tf_op jit(solution)/shard_map/reduce_scatter | solution.py:31
  223.9 108.4 %reduce-scatter.6.cloned.1.call-start = ((), (), s32[]{:S(2)}) async-start(), calls=%async_computation.5 | async-start | bytes 278528 | tf_op jit(solution)/shard_map/reduce_scatter | solution.py:34
  261.9 206.5 %reduce-scatter.8.cloned.1.call-start = ((), (), s32[]{:S(2)}) async-start(), calls=%async_computation.6 | async-start | bytes 14155776 | tf_op jit(solution)/shard_map/reduce_scatter | solution.py:41
  275.2 0.7 copy-start.2
Sparse Core Ops, SparseCore 0:
  224.0 37.8 reduce-scatter.3
  265.6 66.5 reduce-scatter.5
  334.8 133.5 reduce-scatter.7
where the time goes:
time: 479 us; the launch traced here: 477 us
  waiting for transfers between devices  345 us (72%)
  local copies, waits for them, and re-layouts  33.9 us (7%)
  matrix products  32.3 us (7%)
  blocking collectives  23.4 us (5%)
  other arithmetic  21.9 us (5%)
  between operations  13.8 us (3%)
  starting transfers between devices  7.12 us (1%)
    all_to_all x1, waiting for transfers between devices, local(): lax.all_to_all(snapshots, 'tm', split_axis=1, concat_axis=0, tiled=True)  139 us
    reduce_scatter x1, waiting for transfers between devices, local(): lax.psum_scatter(jnp.dot(own_rows.T, local_weighted, preferred_element_ty...  135 us
    reduce_scatter x1, waiting for transfers between devices, local(): lax.psum_scatter(row_sums, 'space', scatter_dimension=0, tiled=True)  56.3 us
    all_gather x1, blocking collectives, local(): all_means = lax.all_gather(mean, 'tm', axis=0, tiled=True)  23.4 us
    dot_general x1, matrix products, gram_local(): lax.dot_general(weighted, weighted, (((1,), (1,)), ((), ())), preferred_e...  19.1 us
    unnamed x7, local copies, waits for them, and re-layouts  17.1 us
    convert_element_type x1, local copies, waits for them, and re-layouts, local(): (own_root[None, :] * (columns.astype(jnp.float32) - mean[None, :])).astyp...  16.7 us
    reduce_scatter x1, waiting for transfers between devices, local(): lax.psum_scatter(partial_gram.astype(jnp.bfloat16), 'tm', scatter_dimensi...  14.6 us
  transfers between devices with their start and end apart: 4, of which 4 were waited for; matrix products, arithmetic and copies ran while one was open for 3% of the time, Pallas kernels for 0%

commit v1 on v0

--- a/solution.py
+++ b/solution.py
@@ -20,7 +20,9 @@
     mode_count = eigvecs.shape[1]
     mode_dev = mode_count // tm_count
     tm_index = lax.axis_index("tm")
-    columns = lax.all_to_all(snapshots, "tm", split_axis=1, concat_axis=0, tiled=True)
+    columns = jnp.concatenate(
+        lax.all_to_all(jnp.stack(jnp.split(snapshots, lax.axis_size("tm"), 1)), "tm", 0, 0), axis=0
+    )
     mean = jnp.sum(columns.astype(jnp.float32), axis=0) / times
     root = jnp.sqrt(area_weight)
     own_root = lax.dynamic_slice_in_dim(root, tm_index * sub_cells, sub_cells, 0)

time: 479 us -> 458 us (0.956)
  local copies, waits for them, and re-layouts: 33.9 us -> 22.5 us
    convert_element_type x1 -> x0, local copies, waits for them, and re-layouts: 16.7 us -> none  [local(): (own_root[None, :] * (columns.astype(jnp.float32) - mean[None, :])).astyp...]
    unnamed x7 -> x13, local copies, waits for them, and re-layouts: 17.1 us -> 19.7 us
where the time goes in v1:
time: 458 us; the launch traced here: 457 us
  waiting for transfers between devices  345 us (75%)
  matrix products  27.7 us (6%)
  blocking collectives  23.4 us (5%)
  local copies, waits for them, and re-layouts  22.5 us (5%)
  other arithmetic  17.7 us (4%)
  between operations  13.8 us (3%)
  starting transfers between devices  7.31 us (2%)
    all_to_all x1, waiting for transfers between devices, local(): lax.all_to_all(jnp.stack(jnp.split(snapshots, lax.axis_size('tm'), 1)), '...  139 us
    reduce_scatter x1, waiting for transfers between devices, local(): lax.psum_scatter(jnp.dot(own_rows.T, local_weighted, preferred_element_ty...  135 us
    reduce_scatter x1, waiting for transfers between devices, local(): lax.psum_scatter(row_sums, 'space', scatter_dimension=0, tiled=True)  56.3 us
    all_gather x1, blocking collectives, local(): all_means = lax.all_gather(mean, 'tm', axis=0, tiled=True)  23.4 us
    unnamed x13, local copies, waits for them, and re-layouts  19.7 us
    reduce_scatter x1, waiting for transfers between devices, local(): lax.psum_scatter(partial_gram.astype(jnp.bfloat16), 'tm', scatter_dimensi...  14.5 us
    dot_general x1, matrix products, gram_local(): lax.dot_general(weighted, weighted, (((1,), (1,)), ((), ())), preferred_e...  14.4 us
    dot_general x1, matrix products, local(): jnp.dot(own_rows.T, local_weighted, preferred_element_type=jnp.float32)  13.2 us
  transfers between devices with their start and end apart: 4, of which 4 were waited for; matrix products, arithmetic and copies ran while one was open for 3% of the time, Pallas kernels for 0%

profile of v1, /device:TPU:1, one launch (start us, length us, event | category | flops | bytes accessed | tf_op | source)
XLA Modules:
  0.0 457.2 jit_solution(7333703687179740057)
XLA Ops:
  7.2 0.0 copy-start
  7.2 2.8 bitcast_dynamic-update-slice_fusion.7
  10.0 2.7 bitcast_dynamic-update-slice_fusion.6
  12.7 2.7 bitcast_dynamic-update-slice_fusion.5
  15.4 2.7 bitcast_dynamic-update-slice_fusion.4
  18.1 2.7 bitcast_dynamic-update-slice_fusion.3
  20.8 2.7 bitcast_dynamic-update-slice_fusion.2
  23.5 2.8 bitcast_dynamic-update-slice_fusion.1
  26.2 2.7 bitcast_dynamic-update-slice_fusion
  28.9 0.0 copy-start.1
  28.9 7.0 %all-to-all-start = ((bf16[8,128,6144]{2,1,0:T(8,128)(2,1)}), bf16[8,128,6144]{2,1,0:T(8,128)(2,1)}, u32[]{:S(2)}, u32[]{:S(2)}) async-start(bf16[8,128,6144]{2,1,0:T(8,128)(2,1)} %bitcast_dynamic-update-slice_fusion), calls=%async_computation | async-start | bytes 25165824 | tf_op jit(solution)/shard_map/all_to_all | solution.py:24
  36.0 0.0 reduce-scatter.4.cloned.1.call-start
  36.0 0.0 copy-done.1
  36.0 0.1 sqrt.6
  36.1 139.1 %all-to-all-done = bf16[8,128,6144]{2,1,0:T(8,128)(2,1)} async-done(((bf16[8,128,6144]{2,1,0:T(8,128)(2,1)}), bf16[8,128,6144]{2,1,0:T(8,128)(2,1)}, u32[]{:S(2)}, u32[]{:S(2)}) %all-to-all-start) | async-done | bytes 12582944 | tf_op jit(solution)/shard_map/all_to_all | solution.py:24
  175.2 6.4 %convert_reduce_fusion = f32[6144]{0:T(1024)S(1)} fusion(bf16[8,128,6144]{2,1,0:T(8,128)(2,1)} %all-to-all-done), kind=kLoop, calls=%fused_computation.1 | loop fusion | flops 12576768 | bytes 12607488 | tf_op jit(solution)/shard_map/reduce_sum | solution.py:26
  181.6 7.5 %fusion.1 = bf16[8,128,6144]{2,1,0:T(8,128)(2,1)S(1)} fusion(bf16[8,128,6144]{2,1,0:T(8,128)(2,1)} %all-to-all-done, f32[6144]{0:T(1024)S(1)} %broadcast_multiply_fusion, f32[6144]{0:T(1024)S(1)} %dynamic_slice.9), kind=kLoop, calls=%fused_computation.3 | loop fusion | flops 25165824 | bytes 25214976 | tf_op jit(solution)/shard_map/convert_element_type | solution.py:29
  189.1 14.4 %multiply_convert_fusion.2 = bf16[1024,1024]{1,0:T(8,128)(2,1)} fusion(bf16[1024,6144]{1,0:T(8,128)(2,1)S(1)} %bitcast.19), kind=kOutput, calls=%fused_computation.8 | convolution fusion | flops 12886999040 | bytes 14680064 | tf_op jit(solution)/shard_map/dot_general | solution.py:8
  203.6 0.0 reduce-scatter.4.cloned.1.call-update
  203.6 0.0 reduce-scatter.6.cloned.1.call-start
  203.6 23.4 %all_gather.3 = f32[49152]{0:T(1024)S(1)} all-gather(f32[6144]{0:T(1024)S(1)} %broadcast_multiply_fusion), channel_id=1, replica_groups=mesh['tm'=8,'space'=16] {'tm'}, dimensions={0}, use_global_device_ids=true | all-gather | bytes 221184 | tf_op jit(solution)/shard_map/all_gather | solution.py:38
  227.0 14.5 %reduce-scatter.4.cloned.1.call-done = bf16[128,1024]{1,0:T(8,128)(2,1)} async-done(((bf16[1024,1024]{1,0:T(8,128)(2,1)}), bf16[128,1024]{1,0:T(8,128)(2,1)}) %reduce-scatter.4.cloned.1.call-update) | async-done | bytes 262160 | tf_op jit(solution)/shard_map/reduce_scatter | solution.py:33
  241.6 0.0 reduce-scatter.6.cloned.1.call-update
  241.6 0.2 reduce-scatter.8.cloned.1.call-start
  241.8 0.0 copy-done
  241.8 13.2 %fusion.2 = f32[64,49152]{1,0:T(8,128)} fusion(bf16[128,49152]{1,0:T(8,128)(2,1)} %param.4, f32[49152]{0:T(1024)S(1)} %all_gather.3, f32[49152]{0:T(1024)S(1)} %sqrt.6, bf16[1024,64]{0,1:T(8,128)(2,1)S(1)} %copy-done, s32[]{:T(128)S(6)} %select_n.10), kind=kOutput, calls=%fused_computation.5 | convolution fusion | flops 830472192 | bytes 25575428 | tf_op jit(solution)/shard_map/dot_general | solution.py:44
  255.1 0.0 copy-start.2
  255.1 0.0 reduce-scatter.8.cloned.1.call-update
  255.1 0.6 copy-done.2
  255.7 0.1 dynamic_slice.11
  255.8 56.3 %reduce-scatter.6.cloned.1.call-done = bf16[8,1024]{1,0:T(8,128)(2,1)} async-done(((bf16[128,1024]{1,0:T(8,128)(2,1)}), bf16[8,1024]{1,0:T(8,128)(2,1)}) %reduce-scatter.6.cloned.1.call-update) | async-done | bytes 16400 | tf_op jit(solution)/shard_map/reduce_scatter | solution.py:36
  312.1 1.3 convert_element_type.33
  313.5 134.8 %reduce-scatter.8.cloned.1.call-done = f32[8,49152]{1,0:T(8,128)} async-done(((f32[64,49152]{1,0:T(8,128)}), f32[8,49152]{1,0:T(8,128)}) %reduce-scatter.8.cloned.1.call-update) | async-done | bytes 1572880 | tf_op jit(solution)/shard_map/reduce_scatter | solution.py:43
  448.3 2.4 multiply_convert_fusion.3
  (3 shorter events, 0.0 us)
Async XLA Ops:
  7.2 234.7 %copy-start = (bf16[1024,64]{0,1:T(8,128)(2,1)S(1)}, bf16[1024,64]{0,1:T(8,128)(2,1)}, u32[]{:S(2)}) copy-start(bf16[1024,64]{0,1:T(8,128)(2,1)} %param.6) | copy-start | bytes 393220
  28.9 7.1 %copy-start.1 = (f32[49152]{0:T(1024)S(1)}, f32[49152]{0:T(1024)}, u32[]{:S(2)}) copy-start(f32[49152]{0:T(1024)} %param.5) | copy-start | bytes 589828
  28.9 146.3 %all-to-all-start = ((bf16[8,128,6144]{2,1,0:T(8,128)(2,1)}), bf16[8,128,6144]{2,1,0:T(8,128)(2,1)}, u32[]{:S(2)}, u32[]{:S(2)}) async-start(bf16[8,128,6144]{2,1,0:T(8,128)(2,1)} %bitcast_dynamic-update-slice_fusion), calls=%async_computation | async-start | bytes 25165824 | tf_op jit(solution)/shard_map/all_to_all | solution.py:24
  36.0 205.6 %reduce-scatter.4.cloned.1.call-start = ((), (), s32[]{:S(2)}) async-start(), calls=%async_computation.4 | async-start | bytes 2359296 | tf_op jit(solution)/shard_map/reduce_scatter | solution.py:33
  203.6 108.6 %reduce-scatter.6.cloned.1.call-start = ((), (), s32[]{:S(2)}) async-start(), calls=%async_computation.5 | async-start | bytes 278528 | tf_op jit(solution)/shard_map/reduce_scatter | solution.py:36
  241.6 206.7 %reduce-scatter.8.cloned.1.call-start = ((), (), s32[]{:S(2)}) async-start(), calls=%async_computation.6 | async-start | bytes 14155776 | tf_op jit(solution)/shard_map/reduce_scatter | solution.py:43
  255.1 0.7 copy-start.2
Sparse Core Ops, SparseCore 0:
  203.7 37.8 reduce-scatter.3
  245.3 66.7 reduce-scatter.5
  314.7 133.5 reduce-scatter.7
